TPU v7x, 512 devices: a whole 4x8x8 slice. The times are simulated.
512 devices in a mesh: pair: 64 (over y, x, core), ka: 8 (over z).
Axes of the slice: x: 4, y: 8, z: 8, core: 2. Of those that a mesh axis runs over, the one named last changes fastest.
Arguments:
- amplitudes: bfloat16 [32768, 4096], P('pair', 'ka'), may hold values from -6 to 6
- tile_mask: int32 [256, 32], P('pair', 'ka'), may hold values 0 or 1
- ladder_ints: bfloat16 [4096, 4096], P('ka', 'pair'), may hold values from -0.09375 to 0.09375
- cycle_right: bfloat16 [32768, 512], P('pair'), may hold values from -0.03125 to 0.03125
- cycle_left: bfloat16 [32768, 512], P('pair'), may hold values from -0.25 to 0.25
Outputs:
- residual: bfloat16 [32768, 4096], P('pair', 'ka')
All inputs are finite; a program needn't handle non-finite values. No bound on the sum of `tile_mask` on one device may be relied on, other than what follows from the above.
Results may differ from a plain program's by a relative error of at most 0.015.
Values may be sent and summed in bfloat16 or wider, within the bound.
A program may use at most 64 MiB of HBM per device.

v0:
```python
import jax
import jax.numpy as jnp
from jax import lax
from jax.sharding import PartitionSpec as P

TB = 128


def body(amplitudes, tile_mask, ladder_ints, cycle_right, cycle_left):
    tiles_row = tile_mask.shape[0]
    tiles_col = tile_mask.shape[1]
    masked = (
        amplitudes.reshape(tiles_row, TB, tiles_col, TB)
        * tile_mask[:, None, :, None].astype(jnp.bfloat16)
    ).reshape(amplitudes.shape)
    partial_hole = lax.dot_general(
        masked, cycle_right, (((0,), (0,)), ((), ())), preferred_element_type=jnp.float32
    )
    hole = lax.psum(partial_hole, "pair").astype(jnp.bfloat16)
    cycle_term = lax.dot_general(
        cycle_left, hole, (((1,), (1,)), ((), ())), preferred_element_type=jnp.float32
    )
    partials = lax.dot_general(
        lax.all_gather(ladder_ints, "pair", axis=1, tiled=True),
        masked,
        (((0,), (1,)), ((), ())),
        preferred_element_type=jnp.float32,
    )
    ladder_owned = lax.psum_scatter(
        partials.astype(jnp.bfloat16), "ka", scatter_dimension=0, tiled=True
    ).astype(jnp.float32)
    return (ladder_owned.T + cycle_term).astype(jnp.bfloat16)


def solution(mesh):
    return jax.shard_map(
        body,
        mesh=mesh,
        in_specs=(
            P("pair", "ka"),
            P("pair", "ka"),
            P("ka", "pair"),
            P("pair", None),
            P("pair", None),
        ),
        out_specs=P("pair", "ka"),
        check_vma=False,
    )
```

profile of v0, /device:TPU:1, one launch (start us, length us, event | category | flops | bytes accessed | tf_op | source)
XLA Modules:
  0.0 370.2 jit_solution(8887892661321940260)
XLA Ops:
  6.5 0.0 copy-start
  6.5 0.0 all-gather.2.cloned.1.call-start
  6.5 0.7 all-gather.2.cloned.1.call-update
  7.3 0.0 reduce-scatter.2.cloned.1.call-start
  7.3 0.7 convert_element_type.22
  8.0 93.0 %all-gather.2.cloned.1.call-done = bf16[512,4096]{0,1:T(8,128)(2,1)} async-done(((bf16[512,64]{0,1:T(8,128)(2,1)}), bf16[512,4096]{0,1:T(8,128)(2,1)}) %all-gather.2.cloned.1.call-update) | async-done | bytes 4194320 | tf_op jit(solution)/shard_map/all_gather | solution.py:24
  101.0 0.2 mul.11
  101.2 6.7 %fusion = bf16[4096,512]{0,1:T(8,128)(2,1)} fusion(bf16[512,4096]{0,1:T(8,128)(2,1)} %all-gather.2.cloned.1.call-done, bf16[512,512]{1,0:T(8,128)(2,1)} %param.5, bf16[64,8,4,128]{3,2,1,0:T(4,128)(2,1)S(1)} %bitcast.14), kind=kOutput, calls=%fused_computation.1 | convolution fusion | flops 2149842944 | bytes 9437184 | tf_op jit(solution)/shard_map/dot_general | solution.py:23
  107.9 0.0 copy-start.1
  107.9 0.0 copy-start.2
  107.9 0.0 reduce-scatter.2.cloned.1.call-update
  107.9 0.0 copy-done
  107.9 1.0 copy-done.1
  108.9 0.5 fusion.4
  109.4 251.6 %all-reduce.1 = bf16[512,512]{1,0:T(8,128)(2,1)S(1)} all-reduce(f32[512,512]{1,0:T(8,128)S(1)} %fusion.4), channel_id=1, replica_groups=mesh['pair'=64,'ka'=8] {'pair'}, use_global_device_ids=true, to_apply=%region_1.0 | all-reduce | flops 262144 | bytes 1572864 | tf_op jit(solution)/shard_map/psum | solution.py:19
  361.0 0.0 reduce-scatter.2.cloned.1.call-done
  361.1 0.0 copy-done.2
  361.1 2.3 fusion.2
Async XLA Ops:
  6.5 101.4 %copy-start = (bf16[512,512]{1,0:T(8,128)(2,1)S(1)}, bf16[512,512]{1,0:T(8,128)(2,1)}, u32[]{:S(2)}) copy-start(bf16[512,512]{1,0:T(8,128)(2,1)} %param.8) | copy-start | bytes 1572868
  6.5 94.5 %all-gather.2.cloned.1.call-start = ((), (), s32[]{:S(2)}) async-start(), calls=%async_computation.1 | async-start | bytes 4259840 | tf_op jit(solution)/shard_map/all_gather | solution.py:24
  7.3 353.8 %reduce-scatter.2.cloned.1.call-start = ((), (), s32[]{:S(2)}) async-start(), calls=%async_computation.2 | async-start | bytes 4718592 | tf_op jit(solution)/shard_map/reduce_scatter | solution.py:29
  107.9 1.0 copy-start.1
  107.9 253.1 %copy-start.2 = (bf16[512,512]{1,0:T(8,128)(2,1)S(1)}, bf16[512,512]{1,0:T(8,128)(2,1)}, u32[]{:S(2)}) copy-start(bf16[512,512]{1,0:T(8,128)(2,1)} %param.9) | copy-start | bytes 1572868
Sparse Core Ops, SparseCore 0:
  10.7 90.2 all-gather.1
  108.1 55.8 reduce-scatter.1
where the time goes:
time: 374 us; the launch traced here: 370 us
  blocking collectives  252 us (67%)
  waiting for transfers between devices  93.8 us (25%)
  between operations  13.4 us (4%)
  matrix products  9.47 us (3%)
    psum x1, blocking collectives, body(): hole = lax.psum(partial_hole, 'pair').astype(jnp.bfloat16)  252 us
    all_gather x1, waiting for transfers between devices, body(): lax.all_gather(ladder_ints, 'pair', axis=1, tiled=True)  93 us
  transfers between devices with their start and end apart: 2, of which 1 were waited for; matrix products, arithmetic and copies ran while one was open for 0% of the time, Pallas kernels for 0%

commit v1 on v0

v1 whole, which is shorter than its diff:
```python
import jax
import jax.numpy as jnp
from jax import lax
from jax.experimental import pallas as pl
from jax.experimental.pallas import tpu as pltpu
from jax.sharding import PartitionSpec as P

MESH = pl.DeviceIdType.MESH
TB = 128
NB = 512
NX, NY, NZ = 4, 8, 8
LC = 64
CH = 128
NCH = NB // CH
HH = NB // 2
HP = HH // NY

bf16, f32 = jnp.bfloat16, jnp.float32
NT = (((1,), (1,)), ((), ()))
TN = (((0,), (0,)), ((), ()))


def kernel(
    mask_ref, amp_hbm, lad_hbm, right_hbm, left_hbm, out_ref,
    amp, lad, right, left, m, lt, la, lb, acc, part, hsend, hx, s1, hy, s2, hxx, hole,
    in_sem, m_ssem, m_rsem, l0_ssem, l0_rsem, l1_ssem, l1_rsem, l2_ssem, l2_rsem, l3_ssem, l3_rsem,
    h1_ssem, h1_rsem, h2_ssem, h2_rsem, h3_ssem, h3_rsem, h4_ssem, h4_rsem, h5_ssem, h5_rsem,
):
    p, z = lax.axis_index("pair"), lax.axis_index("ka")
    c, x, y = p % 2, (p // 2) % NX, p // (2 * NX)
    zt = (y - z + NZ) % NZ

    def dev(dx=0, dy=0, dz=0, dc=0):
        pair = ((y + dy) % NY) * (2 * NX) + ((x + dx) % NX) * 2 + (c + dc) % 2
        return (pair, (z + dz) % NZ)

    def rcopy(src, dst, ssem, rsem, device):
        return pltpu.make_async_remote_copy(
            src_ref=src, dst_ref=dst, send_sem=ssem, recv_sem=rsem, device_id=device, device_id_type=MESH)

    def rows(start, size):
        return pl.ds(pl.multiple_of(start, size), size)

    inputs = [pltpu.make_async_copy(a, b, in_sem.at[i]) for i, (a, b) in enumerate(
        ((amp_hbm, amp), (lad_hbm, lad), (right_hbm, right), (left_hbm, left)))]
    for copy in inputs:
        copy.start()

    barrier = pltpu.get_barrier_semaphore()
    partners = [dev(dz=1), dev(dz=-1), dev(dc=1)] + [dev(dx=d) for d in range(1, NX)] + [dev(dy=d) for d in range(1, NY)]
    for device in partners:
        pl.semaphore_signal(barrier, inc=1, device_id=device, device_id_type=MESH)

    @pl.when(zt != z)
    def _():
        pl.semaphore_signal(barrier, inc=1, device_id=(p, zt), device_id_type=MESH)

    inputs[0].wait()
    for r in range(NB // TB):
        for v in range(NB // TB):
            tile = amp[r * TB:(r + 1) * TB, v * TB:(v + 1) * TB].astype(f32)
            m[0, r * TB:(r + 1) * TB, v * TB:(v + 1) * TB] = (tile * mask_ref[r, v].astype(f32)).astype(bf16)
    pl.semaphore_wait(barrier, len(partners) + (zt != z).astype(jnp.int32))

    def m_copy(up, hop, ch):
        chunk = pl.ds(ch * CH, CH)
        src, dst = ((NZ - hop) % NZ, NZ - 1 - hop) if up else (hop, hop + 1)
        i = hop * NCH + ch
        return rcopy(m.at[src, chunk], m.at[dst, chunk], m_ssem.at[int(up), i], m_rsem.at[int(up), i], dev(dz=1 if up else -1))

    def m_chunks(up, hop):
        if hop < NZ // 2 - 1:
            return range(NCH)
        return range(NCH // 2) if up else range(NCH // 2, NCH)

    m_sent = []

    def m_send(up, hop, ch):
        copy = m_copy(up, hop, ch)
        copy.start()
        m_sent.append(copy)

    def m_forward(hop, ch):
        for up in (True, False):
            m_copy(up, hop - 1, ch).wait_recv()
            if ch in m_chunks(up, hop):
                m_send(up, hop, ch)

    for ch in range(NCH):
        for up in (True, False):
            m_send(up, 0, ch)

    q = 2 * x + c
    inputs[1].wait()
    lt[...] = lad[...].T
    l0a = rcopy(lt, la, l0_ssem.at[0], l0_rsem.at[0], dev(dy=z))
    l0b = rcopy(la, lb.at[z, rows(q * LC, LC)], l0_ssem.at[1], l0_rsem.at[1], (p, zt))

    @pl.when(z != 0)
    def _():
        l0a.start()

    inputs[2].wait()
    part[...] = lax.dot_general(m[0], right[...], TN, preferred_element_type=f32)
    hsend[...] = part[rows((1 - c) * HH, HH), :].astype(bf16)
    h1 = rcopy(hsend, hx, h1_ssem.at[0], h1_rsem.at[0], dev(dc=1))
    h1.start()

    @pl.when(z != 0)
    def _():
        l0a.wait_recv()

    @pl.when(z == 0)
    def _():
        la[...] = lt[...]

    @pl.when(zt != z)
    def _():
        l0b.start()

    @pl.when(zt == z)
    def _():
        lb[z, rows(q * LC, LC), :] = la[...]

    h1.wait_recv()
    s1[...] = (part[rows(c * HH, HH), :] + hx[...].astype(f32)).astype(bf16)
    h2 = []
    for d in range(1, NY):
        there = (y + d) % NY
        h2.append(rcopy(s1.at[rows(there * HP, HP)], hy.at[d], h2_ssem.at[d], h2_rsem.at[d], dev(dy=d)))
        h2[-1].start()

    @pl.when(zt != z)
    def _():
        l0b.wait_recv()

    order = (0, 1, 7, 2, 6, 3, 5, 4)

    def l_place(d):
        return lb.at[(y - d - z + 2 * NZ) % NZ, rows(q * LC, LC)]

    l1 = {}
    for d in order[1:]:
        l1[d] = rcopy(l_place(0), l_place(0), l1_ssem.at[d], l1_rsem.at[d], dev(dy=d))
        l1[d].start()
    l2 = {}

    def l2_send(d):
        for dx in (1, 3, 2):
            l2[d, dx] = rcopy(l_place(d), l_place(d), l2_ssem.at[dx, d], l2_rsem.at[dx, d], dev(dx=dx))
            l2[d, dx].start()

    l2_send(0)
    m_forward(1, 0)
    m_forward(1, 1)
    for d in order[1:3]:
        l1[d].wait_recv()
        l2_send(d)
    m_forward(1, 2)
    for copy in h2:
        copy.wait_recv()
    total = s1[rows(y * HP, HP), :].astype(f32)
    for d in range(1, NY):
        total += hy[d].astype(f32)
    s2[...] = total.astype(bf16)
    h3 = []
    for dx in range(1, NX):
        h3.append(rcopy(s2, hxx.at[dx], h3_ssem.at[dx], h3_rsem.at[dx], dev(dx=dx)))
        h3[-1].start()
    m_forward(1, 3)
    for d in order[3:5]:
        l1[d].wait_recv()
        l2_send(d)
    for copy in h3:
        copy.wait_recv()
    total = s2[...].astype(f32)
    for dx in range(1, NX):
        total += hxx[dx].astype(f32)
    mine = rows(c * HH + y * HP, HP)
    hole[mine, :] = total.astype(bf16)
    h4 = []
    for d in range(1, NY):
        h4.append(rcopy(hole.at[mine], hole.at[mine], h4_ssem.at[d], h4_rsem.at[d], dev(dy=d)))
        h4[-1].start()
    for d in order[5:]:
        l1[d].wait_recv()
        l2_send(d)
    m_forward(2, 0)
    m_forward(2, 1)
    m_forward(2, 2)
    for copy in h4:
        copy.wait_recv()
    half = rows(c * HH, HH)
    h5 = rcopy(hole.at[half], hole.at[half], h5_ssem.at[0], h5_rsem.at[0], dev(dc=1))
    h5.start()
    m_forward(2, 3)
    h5.wait_recv()
    inputs[3].wait()
    acc[...] = lax.dot_general(left[...], hole[...], NT, preferred_element_type=f32)

    l3 = []
    for dx in range(NX):
        if dx:
            for d in order:
                l2[d, dx].wait_recv()
        there = rows((2 * ((x - dx + NX) % NX) + c) * LC, LC)
        l3.append(rcopy(lb.at[:, there], lb.at[:, there], l3_ssem.at[dx], l3_rsem.at[dx], dev(dc=1)))
        l3[-1].start()
    for ch in range(NCH):
        m_forward(3, ch)
    for copy in l3:
        copy.wait_recv()

    @pl.loop(0, NZ - 1)
    def _(i):
        slot = jnp.where(i < NZ // 2, i, i + 1)
        acc[...] += lax.dot_general(m[slot], lb[(z + slot) % NZ], NT, preferred_element_type=f32)

    far = (z + NZ // 2) % NZ
    for i in range(NCH // 2):
        for up, ch in ((True, i), (False, NCH // 2 + i)):
            m_copy(up, NZ // 2 - 1, ch).wait_recv()
            chunk = pl.ds(ch * CH, CH)
            out_ref[chunk, :] = (acc[chunk, :] + lax.dot_general(
                m[NZ // 2, chunk], lb[far], NT, preferred_element_type=f32)).astype(bf16)

    for copy in m_sent + h2 + h3 + h4 + l3 + [h1, h5] + list(l1.values()) + list(l2.values()):
        copy.wait_send()

    @pl.when(z != 0)
    def _():
        l0a.wait_send()

    @pl.when(zt != z)
    def _():
        l0b.wait_send()


def body(amplitudes, tile_mask, ladder_ints, cycle_right, cycle_left):
    dma = pltpu.SemaphoreType.DMA
    pairs = lambda *shape: [dma(shape), dma(shape)]
    return pl.pallas_call(
        kernel,
        out_shape=jax.ShapeDtypeStruct((NB, NB), bf16),
        in_specs=[pl.BlockSpec(memory_space=pltpu.SMEM)] + [pl.BlockSpec(memory_space=pl.ANY)] * 4,
        out_specs=pl.BlockSpec(memory_space=pltpu.VMEM),
        scratch_shapes=[
            pltpu.VMEM((NB, NB), bf16),
            pltpu.VMEM((NB, LC), bf16),
            pltpu.VMEM((NB, NB), bf16),
            pltpu.VMEM((NB, NB), bf16),
            pltpu.VMEM((NZ, NB, NB), bf16),
            pltpu.VMEM((LC, NB), bf16),
            pltpu.VMEM((LC, NB), bf16),
            pltpu.VMEM((NZ, NB, NB), bf16),
            pltpu.VMEM((NB, NB), f32),
            pltpu.VMEM((NB, NB), f32),
            pltpu.VMEM((HH, NB), bf16),
            pltpu.VMEM((HH, NB), bf16),
            pltpu.VMEM((HH, NB), bf16),
            pltpu.VMEM((NY, HP, NB), bf16),
            pltpu.VMEM((HP, NB), bf16),
            pltpu.VMEM((NX, HP, NB), bf16),
            pltpu.VMEM((NB, NB), bf16),
            dma((4,)),
            *pairs(2, NZ // 2 * NCH),
            *pairs(2),
            *pairs(NY),
            *pairs(NX, NY),
            *pairs(NX),
            *pairs(1),
            *pairs(NY),
            *pairs(NX),
            *pairs(NY),
            *pairs(1),
        ],
        compiler_params=pltpu.CompilerParams(
            collective_id=0, has_side_effects=True, vmem_limit_bytes=48 * 2**20),
        cost_estimate=pl.CostEstimate(flops=2 * NB * NB * (NZ * NB + 2 * NB), bytes_accessed=5 * NB * NB * 2, transcendentals=0),
        name="residual_kernel",
    )(tile_mask, amplitudes, ladder_ints, cycle_right, cycle_left)


def solution(mesh):
    return jax.shard_map(
        body,
        mesh=mesh,
        in_specs=(
            P("pair", "ka"),
            P("pair", "ka"),
            P("ka", "pair"),
            P("pair", None),
            P("pair", None),
        ),
        out_specs=P("pair", "ka"),
        check_vma=False,
    )
```

time: 374 us -> 73.9 us (0.20)
  blocking collectives: 252 us -> 0 us
  waiting for transfers between devices: 93.8 us -> 0 us
  Pallas kernels: 0 us -> 68.7 us
  between operations: 13.4 us -> 0.03 us
  matrix products: 9.47 us -> 0 us
    psum x1 -> x0, blocking collectives: 252 us -> none  [body(): hole = lax.psum(partial_hole, 'pair').astype(jnp.bfloat16)]
    all_gather x1 -> x0, waiting for transfers between devices: 93 us -> none  [body(): lax.all_gather(ladder_ints, 'pair', axis=1, tiled=True)]
    pallas_call x0 -> x1, Pallas kernels: none -> 68.7 us  [body(): pl.pallas_call(kernel, out_shape=jax.ShapeDtypeStruct((NB, NB), bf16), in...]
    dot_general x3 -> x0, matrix products: 9.47 us -> none  [the longest x1 6.69 us: body(): lax.dot_general(lax.all_gather(ladder_ints, 'pair', axis=1, tiled=True),...]
    unnamed x6 -> x10, local copies, waits for them, and re-layouts: 1.01 us -> 4.89 us
  transfers between devices with their start and end apart: 2 -> 0, of which waited for: 1 -> 0; matrix products, arithmetic and copies ran while one was open for 0% -> 0% of each run, Pallas kernels for 0% -> 0%
where the time goes in v1:
time: 73.9 us; the launch traced here: 73.6 us
  Pallas kernels  68.7 us (93%)
  local copies, waits for them, and re-layouts  4.89 us (7%)
    pallas_call x1, Pallas kernels, body(): pl.pallas_call(kernel, out_shape=jax.ShapeDtypeStruct((NB, NB), bf16), in...  68.7 us
    unnamed x10, local copies, waits for them, and re-layouts  4.89 us

profile of v1, /device:TPU:1, one launch (start us, length us, event | category | flops | bytes accessed | tf_op | source)
XLA Modules:
  0.0 73.6 jit_solution(6062784003753766951)
XLA Ops:
  0.0 0.0 copy-start.3
  0.0 1.0 %copy.6.lad_hbm = bf16[512,64]{1,0:T(8,128)(2,1)S(1)} copy(bf16[512,64]{0,1:T(8,128)(2,1)} %param.7) | data formatting | bytes 131072 | tf_op args[2]
  1.0 0.0 copy-done.3
  1.0 0.0 copy-start
  1.0 1.0 %copy-done = bf16[512,512]{1,0:T(8,128)(2,1)S(1)} copy-done((bf16[512,512]{1,0:T(8,128)(2,1)S(1)}, bf16[512,512]{1,0:T(8,128)(2,1)}, u32[]{:S(2)}) %copy-start) | copy-done | bytes 524312
  2.0 0.0 copy-start.1
  2.0 1.0 %copy-done.1 = bf16[512,512]{1,0:T(8,128)(2,1)S(1)} copy-done((bf16[512,512]{1,0:T(8,128)(2,1)S(1)}, bf16[512,512]{1,0:T(8,128)(2,1)}, u32[]{:S(2)}) %copy-start.1) | copy-done | bytes 524312
  3.1 0.0 copy-start.2
  3.1 1.0 %copy-done.2 = bf16[512,512]{1,0:T(8,128)(2,1)S(1)} copy-done((bf16[512,512]{1,0:T(8,128)(2,1)S(1)}, bf16[512,512]{1,0:T(8,128)(2,1)}, u32[]{:S(2)}) %copy-start.2) | copy-done | bytes 524312
  4.1 68.7 %residual_kernel.1 = bf16[512,512]{1,0:T(8,128)(2,1)S(1)} custom-call(s32[4,4]{1,0:T(4,128)S(1)} %copy-done.3, bf16[512,512]{1,0:T(8,128)(2,1)S(1)} %copy-done, bf16[512,64]{1,0:T(8,128)(2,1)S(1)} %copy.6.lad_hbm, bf16[512,512]{1,0:T(8,128)(2,1)S(1)} %copy-done.1, bf16[512,512]{1,0:T(8,128)(2,1)S(1)} %copy-done.2), custom_call_target="tpu_custom_call" | custom-call | flops 2684354560 | bytes 2621440 | tf_op jit(solution)/shard_map/residual_kernel/pallas_call | solution.py:242
  72.8 0.8 %copy.8 = bf16[512,512]{1,0:T(8,128)(2,1)} copy(bf16[512,512]{1,0:T(8,128)(2,1)S(1)} %residual_kernel.1) | data formatting | bytes 1048576
Async XLA Ops:
  0.0 1.0 %copy-start.3 = (s32[4,4]{1,0:T(4,128)S(1)}, s32[4,4]{1,0:T(4,128)}, u32[]{:S(2)}) copy-start(s32[4,4]{1,0:T(4,128)} %mask_ref.1) | copy-start | bytes 196
  1.0 1.0 %copy-start = (bf16[512,512]{1,0:T(8,128)(2,1)S(1)}, bf16[512,512]{1,0:T(8,128)(2,1)}, u32[]{:S(2)}) copy-start(bf16[512,512]{1,0:T(8,128)(2,1)} %amp_hbm.1) | copy-start | bytes 1572868
  2.0 1.0 %copy-start.1 = (bf16[512,512]{1,0:T(8,128)(2,1)S(1)}, bf16[512,512]{1,0:T(8,128)(2,1)}, u32[]{:S(2)}) copy-start(bf16[512,512]{1,0:T(8,128)(2,1)} %right_hbm.1) | copy-start | bytes 1572868
  3.1 1.0 %copy-start.2 = (bf16[512,512]{1,0:T(8,128)(2,1)S(1)}, bf16[512,512]{1,0:T(8,128)(2,1)}, u32[]{:S(2)}) copy-start(bf16[512,512]{1,0:T(8,128)(2,1)} %left_hbm.1) | copy-start | bytes 1572868

commit v2 on v0

v2 whole, which is shorter than its diff:
```python
import jax
import jax.numpy as jnp
from jax import lax
from jax.experimental import pallas as pl
from jax.experimental.pallas import tpu as pltpu
from jax.sharding import PartitionSpec as P

MESH = pl.DeviceIdType.MESH
TB = 128
NB = 512
NX, NY, NZ = 4, 8, 8
LC = 64
CH = 64
NCH = NB // CH
EARLY = 6
HH = NB // 2
HP = HH // NY

bf16, f32 = jnp.bfloat16, jnp.float32
NT = (((1,), (1,)), ((), ()))
TN = (((0,), (0,)), ((), ()))


def kernel(
    mask_hbm, amp_hbm, lad_hbm, right_hbm, left_hbm, out_ref,
    mask, amp, lt, right, left, m, la, lb, acc, part, hsend, hx, s1, hy, s2, hxx, hole,
    relay_sem, in_sem, m_ssem, m_rsem, l0_ssem, l0_rsem, l1_ssem, l1_rsem, l2_ssem, l2_rsem, l3_ssem, l3_rsem,
    h1_ssem, h1_rsem, h2_ssem, h2_rsem, h3_ssem, h3_rsem, h4_ssem, h4_rsem, h5_ssem, h5_rsem,
):
    p, z = lax.axis_index("pair"), lax.axis_index("ka")
    c, x, y = p % 2, (p // 2) % NX, p // (2 * NX)
    zt = (y - z + NZ) % NZ

    def dev(dx=0, dy=0, dz=0, dc=0):
        pair = ((y + dy) % NY) * (2 * NX) + ((x + dx) % NX) * 2 + (c + dc) % 2
        return (pair, (z + dz) % NZ)

    def rcopy(src, dst, ssem, rsem, device):
        return pltpu.make_async_remote_copy(
            src_ref=src, dst_ref=dst, send_sem=ssem, recv_sem=rsem, device_id=device, device_id_type=MESH)

    def rows(start, size):
        return pl.ds(pl.multiple_of(start, size), size)

    inputs = [pltpu.make_async_copy(a, b, in_sem.at[i]) for i, (a, b) in enumerate(
        ((amp_hbm, amp), (lad_hbm, lt), (right_hbm, right), (left_hbm, left), (mask_hbm, mask)))]
    for copy in inputs[4:] + inputs[:4]:
        copy.start()

    barrier = pltpu.get_barrier_semaphore()
    neighbours = [dev(dz=1), dev(dz=-1), dev(dc=1), dev(dx=1), dev(dx=-1), dev(dy=1), dev(dy=-1)]
    for device in neighbours:
        pl.semaphore_signal(barrier, inc=1, device_id=device, device_id_type=MESH)

    inputs[4].wait()
    inputs[0].wait()
    for r in range(NB // TB):
        for v in range(NB // TB):
            tile = amp[r * TB:(r + 1) * TB, v * TB:(v + 1) * TB].astype(f32)
            m[0, r * TB:(r + 1) * TB, v * TB:(v + 1) * TB] = (tile * mask[r, v].astype(f32)).astype(bf16)
    pl.semaphore_wait(barrier, len(neighbours))

    def m_rows(up, ch):
        return pl.ds((ch if up else NCH - 1 - ch) * CH, CH)

    def m_copy(up, hop, ch):
        chunk = m_rows(up, ch)
        src, dst = ((NZ - hop) % NZ, NZ - 1 - hop) if up else (hop, hop + 1)
        i = hop * NCH + ch
        return rcopy(m.at[src, chunk], m.at[dst, chunk], m_ssem.at[int(up), i], m_rsem.at[int(up), i], dev(dz=1 if up else -1))

    m_sent = []

    def m_send(up, hop, ch):
        copy = m_copy(up, hop, ch)
        copy.start()
        m_sent.append(copy)

    def m_forward(hop, ch):
        for up in (True, False):
            m_copy(up, hop - 1, ch).wait_recv()
            if hop < NZ // 2 - 1 or ch < NCH // 2:
                m_send(up, hop, ch)

    def m_own(*chunks):
        for ch in chunks:
            for up in (True, False):
                m_send(up, 0, ch)

    m_own(*range(EARLY))

    def relay_signal(r):
        for axis in ("dy", "dz") + ("dx",) * (r == 1):
            for i, d in enumerate((r, -r)):
                pl.semaphore_signal(relay_sem.at["xyz".index(axis[1]), r, i], inc=1, device_id=dev(**{axis: d}), device_id_type=MESH)

    def relay_wait(r):
        for axis in ("dy", "dz") + ("dx",) * (r == 1):
            for i in range(2):
                pl.semaphore_wait(relay_sem.at["xyz".index(axis[1]), r, i], 1)

    l0a = rcopy(lt, la, l0_ssem.at[0], l0_rsem.at[0], dev(dy=z))
    l0b = rcopy(la, lb.at[z, x, c], l0_ssem.at[1], l0_rsem.at[1], (p, zt))

    def l0_first():
        inputs[1].wait()

        @pl.when(z != 0)
        def _():
            l0a.start()

    def l0_second():
        @pl.when(z != 0)
        def _():
            l0a.wait_recv()

        @pl.when(z == 0)
        def _():
            la[...] = lt[...]

        @pl.when(zt != z)
        def _():
            l0b.start()

        @pl.when(zt == z)
        def _():
            lb[z, x, c] = la[...]

    def l_place(d, dx=0):
        return lb.at[(y - d - z + 2 * NZ) % NZ, (x - dx + NX) % NX, c]

    def l1_copy(d):
        step = 1 if d <= NY // 2 else -1
        return rcopy(l_place(d - step), l_place(d - step), l1_ssem.at[d], l1_rsem.at[d], dev(dy=step))

    def l2_copy(d, dx):
        if dx != 2:
            return rcopy(l_place(d), l_place(d), l2_ssem.at[dx, d], l2_rsem.at[dx, d], dev(dx=dx))
        side = 1 if d % 2 else -1
        return rcopy(l_place(d, side), l_place(d, side), l2_ssem.at[dx, d], l2_rsem.at[dx, d], dev(dx=side))

    def l3_copy(d):
        there = lb.at[(y - d - z + 2 * NZ) % NZ, :, c]
        return rcopy(there, there, l3_ssem.at[d], l3_rsem.at[d], dev(dc=1))

    def l0_done():
        @pl.when(zt != z)
        def _():
            l0b.wait_recv()

    def l1_send(d):
        if d:
            l1_copy(d).wait_recv()
        else:
            l0_done()
            l1_copy(NY - 1).start()
        if d < NY // 2:
            l1_copy(d + 1).start()
        if d > NY // 2 + 1:
            l1_copy(d - 1).start()
        l2_copy(d, 1).start()
        l2_copy(d, 3).start()

    def l2_pass(d):
        l2_copy(d, 1 if d % 2 else 3).wait_recv()
        l2_copy(d, 2).start()

    def l3_send(d):
        l2_copy(d, 3 if d % 2 else 1).wait_recv()
        l2_copy(d, 2).wait_recv()
        l3_copy(d).start()

    def l3_done():
        for d in range(NY):
            l3_copy(d).wait_recv()

    def l_sent():
        for d in range(NY):
            if d:
                l1_copy(d).wait_send()
            for dx in range(1, NX):
                l2_copy(d, dx).wait_send()
            l3_copy(d).wait_send()

    def l0_sent():
        @pl.when(z != 0)
        def _():
            l0a.wait_send()

        @pl.when(zt != z)
        def _():
            l0b.wait_send()

    h1 = rcopy(hsend, hx, h1_ssem.at[0], h1_rsem.at[0], dev(dc=1))
    mine = rows(c * HH + y * HP, HP)
    half = rows(c * HH, HH)
    h5 = rcopy(hole.at[half], hole.at[half], h5_ssem.at[0], h5_rsem.at[0], dev(dc=1))

    def h2_copy(d):
        return rcopy(s1.at[rows((y + d) % NY * HP, HP)], hy.at[d], h2_ssem.at[d], h2_rsem.at[d], dev(dy=d))

    def h3_copy(dx):
        return rcopy(s2, hxx.at[dx], h3_ssem.at[dx], h3_rsem.at[dx], dev(dx=dx))

    def h4_copy(d):
        return rcopy(hole.at[mine], hole.at[mine], h4_ssem.at[d], h4_rsem.at[d], dev(dy=d))

    def h1_send():
        inputs[2].wait()
        part[...] = lax.dot_general(m[0], right[...], TN, preferred_element_type=f32)
        hsend[...] = part[rows((1 - c) * HH, HH), :].astype(bf16)
        h1.start()

    def h2_send():
        h1.wait_recv()
        s1[...] = (part[half, :] + hx[...].astype(f32)).astype(bf16)
        for d in range(1, NY):
            h2_copy(d).start()

    def h3_send():
        total = s1[rows(y * HP, HP), :].astype(f32)
        for d in range(1, NY):
            h2_copy(d).wait_recv()
            total += hy[d].astype(f32)
        s2[...] = total.astype(bf16)
        for dx in range(1, NX):
            h3_copy(dx).start()

    def h4_send():
        total = s2[...].astype(f32)
        for dx in range(1, NX):
            h3_copy(dx).wait_recv()
            total += hxx[dx].astype(f32)
        hole[mine, :] = total.astype(bf16)
        for d in range(1, NY):
            h4_copy(d).start()

    def h5_send():
        for d in range(1, NY):
            h4_copy(d).wait_recv()
        h5.start()

    def cycle():
        h5.wait_recv()
        inputs[3].wait()
        acc[...] = lax.dot_general(left[...], hole[...], NT, preferred_element_type=f32)

    def h_sent():
        h1.wait_send()
        for d in range(1, NY):
            h2_copy(d).wait_send()
            h4_copy(d).wait_send()
        for dx in range(1, NX):
            h3_copy(dx).wait_send()
        h5.wait_send()

    def ladder_block(slot):
        return lb[(z + slot) % NZ].reshape(NB, NB)

    def ladder():
        @pl.loop(0, NZ - 1)
        def _(i):
            slot = jnp.where(i < NZ // 2, i, i + 1)
            acc[...] += lax.dot_general(m[slot], ladder_block(slot), NT, preferred_element_type=f32)

    def last():
        block = ladder_block(NZ // 2)
        for ch in range(NCH // 2):
            for up in (True, False):
                m_copy(up, NZ // 2 - 1, ch).wait_recv()
                chunk = m_rows(up, ch)
                out_ref[chunk, :] = (acc[chunk, :] + lax.dot_general(
                    m[NZ // 2, chunk], block, NT, preferred_element_type=f32)).astype(bf16)

    def zm(hop, *chunks):
        for ch in chunks:
            m_forward(hop, ch)

    relay_signal(1)
    h1_send()
    relay_wait(1)
    relay_signal(2)
    relay_wait(2)
    l0_first()
    h2_send()
    l0_second()
    m_own(*range(EARLY, NCH))
    zm(1, 0, 1, 2, 3)
    zm(1, 4)
    l1_send(0)
    zm(1, 5, 6)
    l1_send(1)
    l1_send(7)
    zm(1, 7)
    l2_pass(0)
    l1_send(2)
    l1_send(6)
    zm(2, 0)
    h3_send()
    l2_pass(1)
    l2_pass(7)
    zm(2, 1, 2)
    l1_send(3)
    l1_send(5)
    zm(2, 3)
    l3_send(0)
    l2_pass(2)
    l2_pass(6)
    zm(2, 4)
    l1_send(4)
    h4_send()
    l3_send(1)
    l3_send(7)
    zm(2, 5, 6)
    l2_pass(3)
    l2_pass(5)
    l3_send(2)
    l3_send(6)
    zm(2, 7)
    l2_pass(4)
    zm(3, 0, 1)
    l3_send(3)
    l3_send(5)
    zm(3, 2)
    l3_send(4)
    zm(3, 3)
    h5_send()
    zm(3, 4, 5)
    cycle()
    l3_done()
    zm(3, 6, 7)
    ladder()
    last()
    for copy in m_sent:
        copy.wait_send()
    l0_sent()
    l_sent()
    h_sent()


def body(amplitudes, tile_mask, ladder_ints, cycle_right, cycle_left):
    dma = pltpu.SemaphoreType.DMA
    pairs = lambda *shape: [dma(shape), dma(shape)]
    return pl.pallas_call(
        kernel,
        out_shape=jax.ShapeDtypeStruct((NB, NB), bf16),
        in_specs=[pl.BlockSpec(memory_space=pl.ANY)] * 5,
        out_specs=pl.BlockSpec(memory_space=pltpu.VMEM),
        scratch_shapes=[
            pltpu.SMEM((NB // TB, NB // TB), jnp.int32),
            pltpu.VMEM((NB, NB), bf16),
            pltpu.VMEM((LC, NB), bf16),
            pltpu.VMEM((NB, NB), bf16),
            pltpu.VMEM((NB, NB), bf16),
            pltpu.VMEM((NZ, NB, NB), bf16),
            pltpu.VMEM((LC, NB), bf16),
            pltpu.VMEM((NZ, NX, 2, LC, NB), bf16),
            pltpu.VMEM((NB, NB), f32),
            pltpu.VMEM((NB, NB), f32),
            pltpu.VMEM((HH, NB), bf16),
            pltpu.VMEM((HH, NB), bf16),
            pltpu.VMEM((HH, NB), bf16),
            pltpu.VMEM((NY, HP, NB), bf16),
            pltpu.VMEM((HP, NB), bf16),
            pltpu.VMEM((NX, HP, NB), bf16),
            pltpu.VMEM((NB, NB), bf16),
            pltpu.SemaphoreType.REGULAR((3, 4, 2)),
            dma((5,)),
            *pairs(2, NZ // 2 * NCH),
            *pairs(2),
            *pairs(NY),
            *pairs(NX, NY),
            *pairs(NY),
            *pairs(1),
            *pairs(NY),
            *pairs(NX),
            *pairs(NY),
            *pairs(1),
        ],
        compiler_params=pltpu.CompilerParams(
            collective_id=0, has_side_effects=True, vmem_limit_bytes=63 * 2**20),
        cost_estimate=pl.CostEstimate(flops=2 * NB * NB * (NZ * NB + 2 * NB), bytes_accessed=5 * NB * NB * 2, transcendentals=0),
        name="residual_kernel",
    )(tile_mask, amplitudes, ladder_ints.T, cycle_right, cycle_left)


def solution(mesh):
    return jax.shard_map(
        body,
        mesh=mesh,
        in_specs=(
            P("pair", "ka"),
            P("pair", "ka"),
            P("ka", "pair"),
            P("pair", None),
            P("pair", None),
        ),
        out_specs=P("pair", "ka"),
        check_vma=False,
    )
```

time: 374 us -> 65.3 us (0.17)
  blocking collectives: 252 us -> 0 us
  waiting for transfers between devices: 93.8 us -> 0 us
  Pallas kernels: 0 us -> 63.3 us
  between operations: 13.4 us -> 0.01 us
  matrix products: 9.47 us -> 0 us
    psum x1 -> x0, blocking collectives: 252 us -> none  [body(): hole = lax.psum(partial_hole, 'pair').astype(jnp.bfloat16)]
    all_gather x1 -> x0, waiting for transfers between devices: 93 us -> none  [body(): lax.all_gather(ladder_ints, 'pair', axis=1, tiled=True)]
    pallas_call x0 -> x1, Pallas kernels: none -> 63.3 us  [body(): pl.pallas_call(kernel, out_shape=jax.ShapeDtypeStruct((NB, NB), bf16), in...]
    dot_general x3 -> x0, matrix products: 9.47 us -> none  [the longest x1 6.69 us: body(): lax.dot_general(lax.all_gather(ladder_ints, 'pair', axis=1, tiled=True),...]
  transfers between devices with their start and end apart: 2 -> 0, of which waited for: 1 -> 0; matrix products, arithmetic and copies ran while one was open for 0% -> 0% of each run, Pallas kernels for 0% -> 0%
where the time goes in v2:
time: 65.3 us; the launch traced here: 65.1 us
  Pallas kernels  63.3 us (97%)
  local copies, waits for them, and re-layouts  1.87 us (3%)
    pallas_call x1, Pallas kernels, body(): pl.pallas_call(kernel, out_shape=jax.ShapeDtypeStruct((NB, NB), bf16), in...  63.3 us
    unnamed x1, local copies, waits for them, and re-layouts  1.87 us

profile of v2, /device:TPU:1, one launch (start us, length us, event | category | flops | bytes accessed | tf_op | source)
XLA Modules:
  0.0 65.1 jit_solution(9446429248639373706)
XLA Ops:
  0.0 63.3 %residual_kernel.1 = bf16[512,512]{1,0:T(8,128)(2,1)} custom-call(s32[4,4]{1,0:T(4,128)} %mask_hbm.1, bf16[512,512]{1,0:T(8,128)(2,1)} %amp_hbm.1, bf16[64,512]{1,0:T(8,128)(2,1)} %bitcast.1, bf16[512,512]{1,0:T(8,128)(2,1)} %right_hbm.1, bf16[512,512]{1,0:T(8,128)(2,1)} %left_hbm.1), custom_call_target="tpu_custom_call" | custom-call | flops 2684354560 | bytes 2621440 | tf_op jit(solution)/shard_map/residual_kernel/pallas_call | solution.py:344
  63.3 1.9 %copy.7 = bf16[512,512]{1,0:T(8,128)(2,1)} copy(bf16[512,512]{1,0:T(8,128)(2,1)} %residual_kernel.1) | data formatting | bytes 1048576

commit v3 on v2

v3 whole, which is shorter than its diff:
```python
import jax
import jax.numpy as jnp
from jax import lax
from jax.experimental import pallas as pl
from jax.experimental.pallas import tpu as pltpu
from jax.sharding import PartitionSpec as P

MESH = pl.DeviceIdType.MESH
TB = 128
NB = 512
NX, NY, NZ = 4, 8, 8
LC = 64
CH = 128
NCH = NB // CH
EARLY = 2
HH = NB // 2
HP = HH // NY

bf16, f32 = jnp.bfloat16, jnp.float32
NT = (((1,), (1,)), ((), ()))
TN = (((0,), (0,)), ((), ()))


def kernel(
    mask_hbm, amp_hbm, lad_hbm, right_hbm, left_hbm, out_hbm,
    mask, amp, lt, right, left, m, la, lb, acc, part, hsend, hx, s1, hy, s2, hxx, hole, out,
    ack, in_sem, out_sem, m_ssem, m_rsem, l0_ssem, l0_rsem, l1_ssem, l1_rsem, l2_ssem, l2_rsem, l3_ssem, l3_rsem,
    h1_ssem, h1_rsem, h2_ssem, h2_rsem, h3_ssem, h3_rsem, h4_ssem, h4_rsem, h5_ssem, h5_rsem,
):
    p, z = lax.axis_index("pair"), lax.axis_index("ka")
    c, x, y = p % 2, (p // 2) % NX, p // (2 * NX)
    zt = (y - z + NZ) % NZ

    def dev(dx=0, dy=0, dz=0, dc=0):
        pair = ((y + dy) % NY) * (2 * NX) + ((x + dx) % NX) * 2 + (c + dc) % 2
        return (pair, (z + dz) % NZ)

    def rcopy(src, dst, ssem, rsem, device):
        return pltpu.make_async_remote_copy(
            src_ref=src, dst_ref=dst, send_sem=ssem, recv_sem=rsem, device_id=device, device_id_type=MESH)

    def drain(ref, sem):
        pltpu.make_async_copy(ref, ref, sem).wait()

    def rows(start, size):
        return pl.ds(pl.multiple_of(start, size), size)

    mask_in = pltpu.make_async_copy(mask_hbm, mask, in_sem.at[0])
    inputs = [pltpu.make_async_copy(a, b, in_sem.at[1 + i]) for i, (a, b) in enumerate(
        ((lad_hbm, lt), (right_hbm, right), (left_hbm, left)))]
    amp_in = [pltpu.make_async_copy(amp_hbm.at[pl.ds(i * CH, CH)], amp.at[pl.ds(i * CH, CH)], in_sem.at[4 + i]) for i in range(NCH)]
    from_ends = [i for j in range(NCH // 2) for i in (j, NCH - 1 - j)]
    mask_in.start()
    amp_in[from_ends[0]].start()
    amp_in[from_ends[1]].start()

    def rank(v):
        return jnp.where(v <= NY // 2, 2 * v, 2 * (NY - v) + 1)

    partners = {
        ("z", 1): (dev(dz=1), (z + 1) % NZ > z, None, ("z", -1)),
        ("z", -1): (dev(dz=-1), (z + NZ - 1) % NZ > z, None, ("z", 1)),
        ("t", 0): ((p, zt), zt > z, zt != z, ("t", 0)),
        ("c", 1): (dev(dc=1), c == 1, None, ("c", 1)),
    }
    for d in range(1, NX):
        partners["x", d] = (dev(dx=d), (x + d) % NX > x, None, ("x", NX - d))
    for d in range(1, NY):
        partners["y", d] = (dev(dy=d), rank((y + d) % NY) > rank(y), None, ("y", NY - d))
    ack_of = {name: i for i, name in enumerate(partners)}

    barrier = pltpu.get_barrier_semaphore()
    earlier = 0
    for device, later, valid, _ in partners.values():
        @pl.when(later)
        def _():
            pl.semaphore_signal(barrier, inc=1, device_id=device, device_id_type=MESH)

        before = jnp.logical_not(later)
        if valid is not None:
            before = jnp.logical_and(before, valid)
        earlier += before.astype(jnp.int32)

    def answer():
        @pl.when(earlier > 0)
        def _():
            pl.semaphore_wait(barrier, earlier)

        for device, later, valid, there in partners.values():
            before = jnp.logical_not(later)
            if valid is not None:
                before = jnp.logical_and(before, valid)

            @pl.when(before)
            def _():
                pl.semaphore_signal(ack.at[ack_of[there]], inc=1, device_id=device, device_id_type=MESH)

    def met(axis):
        for name, (_, later, _, _) in partners.items():
            if name[0] == axis:
                @pl.when(later)
                def _():
                    pl.semaphore_wait(ack.at[ack_of[name]], 1)

    for i in from_ends[2:]:
        amp_in[i].start()
    for copy in inputs:
        copy.start()

    def masked(i):
        amp_in[i].wait()
        for v in range(NB // TB):
            here = (slice(i * CH, (i + 1) * CH), slice(v * TB, (v + 1) * TB))
            m[(0, *here)] = (amp[here].astype(f32) * mask[i * CH // TB, v].astype(f32)).astype(bf16)

    mask_in.wait()
    masked(from_ends[0])
    masked(from_ends[1])
    answer()
    met("z")

    def m_rows(up, ch):
        return pl.ds((ch if up else NCH - 1 - ch) * CH, CH)

    def m_copy(up, hop, ch):
        chunk = m_rows(up, ch)
        src, dst = ((NZ - hop) % NZ, NZ - 1 - hop) if up else (hop, hop + 1)
        i = hop * NCH + ch
        return rcopy(m.at[src, chunk], m.at[dst, chunk], m_ssem.at[0], m_rsem.at[int(up), i], dev(dz=1 if up else -1))

    def m_send(up, hop, ch):
        m_copy(up, hop, ch).start()

    def m_forward(hop, ch):
        for up in (True, False):
            m_copy(up, hop - 1, ch).wait_recv()
            if hop < NZ // 2 - 1 or ch < NCH // 2:
                m_send(up, hop, ch)

    def m_own(*chunks):
        for ch in chunks:
            for up in (True, False):
                m_send(up, 0, ch)

    m_own(0)
    for i in range(1, NCH // 2):
        masked(from_ends[2 * i])
        masked(from_ends[2 * i + 1])
        if i < EARLY:
            m_own(i)
    m_own(*range(NCH // 2, EARLY))

    l0a = rcopy(lt, la, l0_ssem.at[0], l0_rsem.at[0], dev(dy=z))
    l0b = rcopy(la, lb.at[z, x, c], l0_ssem.at[1], l0_rsem.at[1], (p, zt))

    def l0_first():
        inputs[0].wait()

        @pl.when(z != 0)
        def _():
            l0a.start()

    def l0_second():
        @pl.when(z != 0)
        def _():
            l0a.wait_recv()

        @pl.when(z == 0)
        def _():
            la[...] = lt[...]

        @pl.when(zt != z)
        def _():
            l0b.start()

        @pl.when(zt == z)
        def _():
            lb[z, x, c] = la[...]

    def l_place(d, dx=0):
        return lb.at[(y - d - z + 2 * NZ) % NZ, (x - dx + NX) % NX, c]

    def l1_copy(d):
        if d == NY // 2:
            src, step = l_place(jnp.where(c == 0, 2, NY - 2)), jnp.where(c == 0, 2, NY - 2)
        else:
            step = {1: 1, 2: 2, 3: 1, 5: NY - 1, 6: NY - 2, 7: NY - 1}[d]
            src = l_place((d - step + NY) % NY)
        return rcopy(src, src, l1_ssem.at[0], l1_rsem.at[d], dev(dy=step))

    def l2_copy(d, dx):
        side = 1 if d % 2 else NX - 1
        src, step = (l_place(d, side), side) if dx == 2 else (l_place(d), dx)
        return rcopy(src, src, l2_ssem.at[0], l2_rsem.at[0 if dx == side else 1, d], dev(dx=step))

    def l3_copy(d):
        there = lb.at[(y - d - z + 2 * NZ) % NZ, :, c]
        return rcopy(there, there, l3_ssem.at[0], l3_rsem.at[0], dev(dc=1))

    def l0_done():
        @pl.when(zt != z)
        def _():
            l0b.wait_recv()

    def l1_send(d):
        if d:
            l1_copy(d).wait_recv()
        else:
            l0_done()
        for further in {0: (1, 7, 2, 6), 2: (3,), 6: (5, 4)}.get(d, ()):
            l1_copy(further).start()
        l2_copy(d, 1).start()
        l2_copy(d, 3).start()

    def l2_pass(d):
        l2_copy(d, 1 if d % 2 else 3).wait_recv()
        l2_copy(d, 2).start()

    def l3_send(d):
        drain(lb.at[0, pl.ds(0, 2), 0], l2_rsem.at[1, d])
        l3_copy(d).start()

    def l3_done():
        drain(lb.at[:, :, 0], l3_rsem.at[0])

    def l_sent():
        drain(lb.at[pl.ds(0, NY - 1), 0, 0], l1_ssem.at[0])
        drain(lb.at[:, pl.ds(0, NX - 1), 0], l2_ssem.at[0])
        drain(lb.at[:, :, 0], l3_ssem.at[0])

    def l0_sent():
        @pl.when(z != 0)
        def _():
            l0a.wait_send()

        @pl.when(zt != z)
        def _():
            l0b.wait_send()

    h1 = rcopy(hsend, hx, h1_ssem.at[0], h1_rsem.at[0], dev(dc=1))
    mine = rows(c * HH + y * HP, HP)
    half = rows(c * HH, HH)
    h5 = rcopy(hole.at[half], hole.at[half], h5_ssem.at[0], h5_rsem.at[0], dev(dc=1))

    def h2_copy(d):
        return rcopy(s1.at[rows((y + d) % NY * HP, HP)], hy.at[d], h2_ssem.at[0], h2_rsem.at[0], dev(dy=d))

    def h3_copy(dx):
        return rcopy(s2, hxx.at[dx], h3_ssem.at[0], h3_rsem.at[0], dev(dx=dx))

    def h4_copy(d):
        return rcopy(hole.at[mine], hole.at[mine], h4_ssem.at[0], h4_rsem.at[0], dev(dy=d))

    def h1_send():
        inputs[1].wait()
        part[...] = lax.dot_general(m[0], right[...], TN, preferred_element_type=f32)
        hsend[...] = part[rows((1 - c) * HH, HH), :].astype(bf16)
        h1.start()

    def h2_send():
        h1.wait_recv()
        s1[...] = (part[half, :] + hx[...].astype(f32)).astype(bf16)
        for d in range(1, NY):
            h2_copy(d).start()

    def h3_send():
        drain(hy.at[pl.ds(1, NY - 1)], h2_rsem.at[0])
        total = s1[rows(y * HP, HP), :].astype(f32)
        for d in range(1, NY):
            total += hy[d].astype(f32)
        s2[...] = total.astype(bf16)
        for dx in range(1, NX):
            h3_copy(dx).start()

    def h4_send():
        drain(hxx.at[pl.ds(1, NX - 1)], h3_rsem.at[0])
        total = s2[...].astype(f32)
        for dx in range(1, NX):
            total += hxx[dx].astype(f32)
        hole[mine, :] = total.astype(bf16)
        for d in range(1, NY):
            h4_copy(d).start()

    def h5_send():
        drain(hy.at[pl.ds(1, NY - 1)], h4_rsem.at[0])
        h5.start()

    def cycle():
        h5.wait_recv()
        inputs[2].wait()
        acc[...] = lax.dot_general(left[...], hole[...], NT, preferred_element_type=f32)

    def h_sent():
        h1.wait_send()
        drain(hy.at[pl.ds(1, NY - 1)], h2_ssem.at[0])
        drain(hxx.at[pl.ds(1, NX - 1)], h3_ssem.at[0])
        drain(hy.at[pl.ds(1, NY - 1)], h4_ssem.at[0])
        h5.wait_send()

    def ladder_block(slot):
        return lb[(z + slot) % NZ].reshape(NB, NB)

    def ladder(n, first, step):
        @pl.loop(0, n)
        def _(i):
            slot = (first + step * i) % NZ
            acc[...] += lax.dot_general(m[slot], ladder_block(slot), NT, preferred_element_type=f32)

    def last():
        block = ladder_block(NZ // 2)
        for ch in range(NCH // 2):
            for up in (True, False):
                m_copy(up, NZ // 2 - 1, ch).wait_recv()
                chunk = m_rows(up, ch)
                out[chunk, :] = (acc[chunk, :] + lax.dot_general(
                    m[NZ // 2, chunk], block, NT, preferred_element_type=f32)).astype(bf16)
                pltpu.make_async_copy(out.at[chunk], out_hbm.at[chunk], out_sem.at[0]).start()

    def zm(hop, *chunks):
        for ch in chunks:
            m_forward(hop, ch)

    met("y")
    l0_first()
    met("c")
    h1_send()
    h2_send()
    zm(1, 0)
    met("t")
    l0_second()
    m_own(*range(EARLY, NCH))
    zm(1, 1)
    met("x")
    l1_send(0)
    zm(1, 2)
    l1_send(1)
    l1_send(7)
    l2_pass(0)
    l1_send(2)
    l1_send(6)
    zm(1, 3)
    h3_send()
    l2_pass(1)
    l2_pass(7)
    zm(2, 0)
    l1_send(3)
    l1_send(5)
    l3_send(0)
    l1_send(4)
    l2_pass(2)
    l2_pass(6)
    zm(2, 1)
    h4_send()
    l3_send(1)
    l3_send(7)
    l2_pass(3)
    l2_pass(5)
    l2_pass(4)
    zm(2, 2)
    l3_send(2)
    l3_send(6)
    zm(2, 3)
    l3_send(3)
    l3_send(5)
    l3_send(4)
    h5_send()
    zm(3, 0)
    cycle()
    zm(3, 1)
    l3_done()
    ladder(5, 6, 1)
    zm(3, 2, 3)
    ladder(2, 3, 2)
    last()
    drain(out, out_sem.at[0])
    drain(m.at[pl.ds(0, NZ - 1)], m_ssem.at[0])
    l0_sent()
    l_sent()
    h_sent()


def body(amplitudes, tile_mask, ladder_ints, cycle_right, cycle_left):
    dma = pltpu.SemaphoreType.DMA
    return pl.pallas_call(
        kernel,
        out_shape=jax.ShapeDtypeStruct((NB, NB), bf16),
        in_specs=[pl.BlockSpec(memory_space=pl.ANY)] * 5,
        out_specs=pl.BlockSpec(memory_space=pl.ANY),
        scratch_shapes=[
            pltpu.SMEM((NB // TB, NB // TB), jnp.int32),
            pltpu.VMEM((NB, NB), bf16),
            pltpu.VMEM((LC, NB), bf16),
            pltpu.VMEM((NB, NB), bf16),
            pltpu.VMEM((NB, NB), bf16),
            pltpu.VMEM((NZ, NB, NB), bf16),
            pltpu.VMEM((LC, NB), bf16),
            pltpu.VMEM((NZ, NX, 2, LC, NB), bf16),
            pltpu.VMEM((NB, NB), f32),
            pltpu.VMEM((NB, NB), f32),
            pltpu.VMEM((HH, NB), bf16),
            pltpu.VMEM((HH, NB), bf16),
            pltpu.VMEM((HH, NB), bf16),
            pltpu.VMEM((NY, HP, NB), bf16),
            pltpu.VMEM((HP, NB), bf16),
            pltpu.VMEM((NX, HP, NB), bf16),
            pltpu.VMEM((NB, NB), bf16),
            pltpu.VMEM((NB, NB), bf16),
            pltpu.SemaphoreType.REGULAR((4 + NX - 1 + NY - 1,)),
            dma((4 + NCH,)),
            dma((1,)),
            dma((1,)), dma((2, NZ // 2 * NCH - NCH // 2)),
            dma((2,)), dma((2,)),
            dma((1,)), dma((NY,)),
            dma((1,)), dma((2, NY)),
            dma((1,)), dma((1,)),
            *[dma((1,))] * 10,
        ],
        compiler_params=pltpu.CompilerParams(
            collective_id=0, has_side_effects=True, vmem_limit_bytes=64 * 2**20),
        cost_estimate=pl.CostEstimate(flops=2 * NB * NB * (NZ * NB + 2 * NB), bytes_accessed=5 * NB * NB * 2, transcendentals=0),
        name="residual_kernel",
    )(tile_mask, amplitudes, ladder_ints.T, cycle_right, cycle_left)


def solution(mesh):
    return jax.shard_map(
        body,
        mesh=mesh,
        in_specs=(
            P("pair", "ka"),
            P("pair", "ka"),
            P("ka", "pair"),
            P("pair", None),
            P("pair", None),
        ),
        out_specs=P("pair", "ka"),
        check_vma=False,
    )
```

time: 65.3 us -> 63.2 us (0.968)
  Pallas kernels: 63.3 us -> 61.2 us
    pallas_call x1, Pallas kernels: 63.3 us -> 61.2 us  [body(): pl.pallas_call(kernel, out_shape=jax.ShapeDtypeStruct((NB, NB), bf16), in...]
where the time goes in v3:
time: 63.2 us; the launch traced here: 63 us
  Pallas kernels  61.2 us (97%)
  local copies, waits for them, and re-layouts  1.87 us (3%)
    pallas_call x1, Pallas kernels, body(): pl.pallas_call(kernel, out_shape=jax.ShapeDtypeStruct((NB, NB), bf16), in...  61.2 us
    unnamed x1, local copies, waits for them, and re-layouts  1.87 us

profile of v3, /device:TPU:1, one launch (start us, length us, event | category | flops | bytes accessed | tf_op | source)
XLA Modules:
  0.0 63.0 jit_solution(15317845596091624954)
XLA Ops:
  0.0 61.2 %residual_kernel.1 = bf16[512,512]{1,0:T(8,128)(2,1)} custom-call(s32[4,4]{1,0:T(4,128)} %mask_hbm.1, bf16[512,512]{1,0:T(8,128)(2,1)} %amp_hbm.1, bf16[64,512]{1,0:T(8,128)(2,1)} %bitcast.1, bf16[512,512]{1,0:T(8,128)(2,1)} %right_hbm.1, bf16[512,512]{1,0:T(8,128)(2,1)} %left_hbm.1), custom_call_target="tpu_custom_call" | custom-call | flops 2684354560 | bytes 2621440 | tf_op jit(solution)/shard_map/residual_kernel/pallas_call | solution.py:384
  61.2 1.9 %copy.7 = bf16[512,512]{1,0:T(8,128)(2,1)} copy(bf16[512,512]{1,0:T(8,128)(2,1)} %residual_kernel.1) | data formatting | bytes 1048576

commit v4 on v3

--- a/solution.py
+++ b/solution.py
@@ -12,9 +12,11 @@
 LC = 64
 CH = 128
 NCH = NB // CH
+BESIDE = (1, NY - 1)
 EARLY = 2
 HH = NB // 2
-HP = HH // NY
+HQ = HH // NX
+HP, HW = HQ // 4, NB // 2
 
 bf16, f32 = jnp.bfloat16, jnp.float32
 NT = (((1,), (1,)), ((), ()))
@@ -25,7 +27,7 @@
     mask_hbm, amp_hbm, lad_hbm, right_hbm, left_hbm, out_hbm,
     mask, amp, lt, right, left, m, la, lb, acc, part, hsend, hx, s1, hy, s2, hxx, hole, out,
     ack, in_sem, out_sem, m_ssem, m_rsem, l0_ssem, l0_rsem, l1_ssem, l1_rsem, l2_ssem, l2_rsem, l3_ssem, l3_rsem,
-    h1_ssem, h1_rsem, h2_ssem, h2_rsem, h3_ssem, h3_rsem, h4_ssem, h4_rsem, h5_ssem, h5_rsem,
+    h1_ssem, h1_rsem, h2_ssem, h2_rsem, h3_ssem, h3_rsem, h4_ssem, h4_rsem, h5_ssem, h5_rsem, h6_ssem, h6_rsem,
 ):
     p, z = lax.axis_index("pair"), lax.axis_index("ka")
     c, x, y = p % 2, (p // 2) % NX, p // (2 * NX)
@@ -193,6 +195,9 @@
         src, step = (l_place(d, side), side) if dx == 2 else (l_place(d), dx)
         return rcopy(src, src, l2_ssem.at[0], l2_rsem.at[0 if dx == side else 1, d], dev(dx=step))
 
+    def l2_beside(d, dx):
+        return rcopy(l_place(0, dx), l_place(0, dx), l2_ssem.at[0], l2_rsem.at[1, d], dev(dy=d))
+
     def l3_copy(d):
         there = lb.at[(y - d - z + 2 * NZ) % NZ, :, c]
         return rcopy(there, there, l3_ssem.at[0], l3_rsem.at[0], dev(dc=1))
@@ -209,16 +214,21 @@
             l0_done()
         for further in {0: (1, 7, 2, 6), 2: (3,), 6: (5, 4)}.get(d, ()):
             l1_copy(further).start()
-        l2_copy(d, 1).start()
-        l2_copy(d, 3).start()
+        if d not in BESIDE:
+            l2_copy(d, 1).start()
+            l2_copy(d, 3).start()
 
     def l2_pass(d):
         l2_copy(d, 1 if d % 2 else 3).wait_recv()
         l2_copy(d, 2).start()
 
     def l3_send(d):
-        drain(lb.at[0, pl.ds(0, 2), 0], l2_rsem.at[1, d])
+        drain(lb.at[0, pl.ds(0, 3 if d in BESIDE else 2), 0], l2_rsem.at[1, d])
         l3_copy(d).start()
+        if d == 0:
+            for beside in BESIDE:
+                for dx in range(1, NX):
+                    l2_beside(beside, dx).start()
 
     def l3_done():
         drain(lb.at[:, :, 0], l3_rsem.at[0])
@@ -238,18 +248,26 @@
             l0b.wait_send()
 
     h1 = rcopy(hsend, hx, h1_ssem.at[0], h1_rsem.at[0], dev(dc=1))
-    mine = rows(c * HH + y * HP, HP)
     half = rows(c * HH, HH)
-    h5 = rcopy(hole.at[half], hole.at[half], h5_ssem.at[0], h5_rsem.at[0], dev(dc=1))
-
-    def h2_copy(d):
-        return rcopy(s1.at[rows((y + d) % NY * HP, HP)], hy.at[d], h2_ssem.at[0], h2_rsem.at[0], dev(dy=d))
-
-    def h3_copy(dx):
-        return rcopy(s2, hxx.at[dx], h3_ssem.at[0], h3_rsem.at[0], dev(dx=dx))
+    quarter = rows(c * HH + x * HQ, HQ)
+    h6 = rcopy(hole.at[half], hole.at[half], h6_ssem.at[0], h6_rsem.at[0], dev(dc=1))
+
+    def piece(v):
+        return rows(v // 2 * HP, HP), rows(v % 2 * HW, HW)
+
+    mine = (rows(c * HH + x * HQ + y // 2 * HP, HP), rows(y % 2 * HW, HW))
+
+    def h2_copy(dx):
+        return rcopy(s1.at[rows((x + dx) % NX * HQ, HQ)], hxx.at[dx], h2_ssem.at[0], h2_rsem.at[0], dev(dx=dx))
+
+    def h3_copy(d):
+        return rcopy(s2.at[piece((y + d) % NY)], hy.at[d], h3_ssem.at[0], h3_rsem.at[0], dev(dy=d))
 
     def h4_copy(d):
         return rcopy(hole.at[mine], hole.at[mine], h4_ssem.at[0], h4_rsem.at[0], dev(dy=d))
+
+    def h5_copy(dx):
+        return rcopy(hole.at[quarter], hole.at[quarter], h5_ssem.at[0], h5_rsem.at[0], dev(dx=dx))
 
     def h1_send():
         inputs[1].wait()
@@ -260,42 +278,48 @@
     def h2_send():
         h1.wait_recv()
         s1[...] = (part[half, :] + hx[...].astype(f32)).astype(bf16)
+        for dx in range(1, NX):
+            h2_copy(dx).start()
+
+    def h3_send():
+        drain(hxx.at[pl.ds(1, NX - 1)], h2_rsem.at[0])
+        total = s1[rows(x * HQ, HQ), :].astype(f32)
+        for dx in range(1, NX):
+            total += hxx[dx].astype(f32)
+        s2[...] = total.astype(bf16)
         for d in range(1, NY):
-            h2_copy(d).start()
-
-    def h3_send():
-        drain(hy.at[pl.ds(1, NY - 1)], h2_rsem.at[0])
-        total = s1[rows(y * HP, HP), :].astype(f32)
+            h3_copy(d).start()
+
+    def h4_send():
+        drain(hy.at[pl.ds(1, NY - 1)], h3_rsem.at[0])
+        total = s2[piece(y)].astype(f32)
         for d in range(1, NY):
             total += hy[d].astype(f32)
-        s2[...] = total.astype(bf16)
-        for dx in range(1, NX):
-            h3_copy(dx).start()
-
-    def h4_send():
-        drain(hxx.at[pl.ds(1, NX - 1)], h3_rsem.at[0])
-        total = s2[...].astype(f32)
-        for dx in range(1, NX):
-            total += hxx[dx].astype(f32)
-        hole[mine, :] = total.astype(bf16)
+        hole[mine] = total.astype(bf16)
         for d in range(1, NY):
             h4_copy(d).start()
 
     def h5_send():
         drain(hy.at[pl.ds(1, NY - 1)], h4_rsem.at[0])
-        h5.start()
+        for dx in range(1, NX):
+            h5_copy(dx).start()
+
+    def h6_send():
+        drain(hxx.at[pl.ds(1, NX - 1)], h5_rsem.at[0])
+        h6.start()
 
     def cycle():
-        h5.wait_recv()
+        h6.wait_recv()
         inputs[2].wait()
         acc[...] = lax.dot_general(left[...], hole[...], NT, preferred_element_type=f32)
 
     def h_sent():
         h1.wait_send()
-        drain(hy.at[pl.ds(1, NY - 1)], h2_ssem.at[0])
-        drain(hxx.at[pl.ds(1, NX - 1)], h3_ssem.at[0])
+        drain(hxx.at[pl.ds(1, NX - 1)], h2_ssem.at[0])
+        drain(hy.at[pl.ds(1, NY - 1)], h3_ssem.at[0])
         drain(hy.at[pl.ds(1, NY - 1)], h4_ssem.at[0])
-        h5.wait_send()
+        drain(hxx.at[pl.ds(1, NX - 1)], h5_ssem.at[0])
+        h6.wait_send()
 
     def ladder_block(slot):
         return lb[(z + slot) % NZ].reshape(NB, NB)
@@ -324,49 +348,48 @@
     l0_first()
     met("c")
     h1_send()
-    h2_send()
     zm(1, 0)
     met("t")
     l0_second()
     m_own(*range(EARLY, NCH))
+    met("x")
+    h2_send()
     zm(1, 1)
-    met("x")
+    h3_send()
     l1_send(0)
     zm(1, 2)
-    l1_send(1)
-    l1_send(7)
-    l2_pass(0)
     l1_send(2)
     l1_send(6)
+    l2_pass(0)
     zm(1, 3)
-    h3_send()
-    l2_pass(1)
-    l2_pass(7)
+    h4_send()
+    l3_send(0)
     zm(2, 0)
     l1_send(3)
     l1_send(5)
-    l3_send(0)
     l1_send(4)
     l2_pass(2)
+    zm(2, 1)
     l2_pass(6)
-    zm(2, 1)
-    h4_send()
-    l3_send(1)
-    l3_send(7)
+    h5_send()
+    l1_send(1)
+    l1_send(7)
     l2_pass(3)
     l2_pass(5)
     l2_pass(4)
     zm(2, 2)
+    l3_send(1)
+    l3_send(7)
     l3_send(2)
     l3_send(6)
     zm(2, 3)
+    h6_send()
     l3_send(3)
     l3_send(5)
     l3_send(4)
-    h5_send()
     zm(3, 0)
+    zm(3, 1)
     cycle()
-    zm(3, 1)
     l3_done()
     ladder(5, 6, 1)
     zm(3, 2, 3)
@@ -400,9 +423,9 @@
             pltpu.VMEM((HH, NB), bf16),
             pltpu.VMEM((HH, NB), bf16),
             pltpu.VMEM((HH, NB), bf16),
-            pltpu.VMEM((NY, HP, NB), bf16),
-            pltpu.VMEM((HP, NB), bf16),
-            pltpu.VMEM((NX, HP, NB), bf16),
+            pltpu.VMEM((NY, HP, HW), bf16),
+            pltpu.VMEM((HQ, NB), bf16),
+            pltpu.VMEM((NX, HQ, NB), bf16),
             pltpu.VMEM((NB, NB), bf16),
             pltpu.VMEM((NB, NB), bf16),
             pltpu.SemaphoreType.REGULAR((4 + NX - 1 + NY - 1,)),
@@ -413,7 +436,7 @@
             dma((1,)), dma((NY,)),
             dma((1,)), dma((2, NY)),
             dma((1,)), dma((1,)),
-            *[dma((1,))] * 10,
+            *[dma((1,))] * 12,
         ],
         compiler_params=pltpu.CompilerParams(
             collective_id=0, has_side_effects=True, vmem_limit_bytes=64 * 2**20),

time: 63.2 us -> 60.9 us (0.964)
  Pallas kernels: 61.2 us -> 58.8 us
    pallas_call x1, Pallas kernels: 61.2 us -> 58.8 us  [body(): pl.pallas_call(kernel, out_shape=jax.ShapeDtypeStruct((NB, NB), bf16), in...]
where the time goes in v4:
time: 60.9 us; the launch traced here: 60.7 us
  Pallas kernels  58.8 us (97%)
  local copies, waits for them, and re-layouts  1.87 us (3%)
    pallas_call x1, Pallas kernels, body(): pl.pallas_call(kernel, out_shape=jax.ShapeDtypeStruct((NB, NB), bf16), in...  58.8 us
    unnamed x1, local copies, waits for them, and re-layouts  1.87 us

profile of v4, /device:TPU:1, one launch (start us, length us, event | category | flops | bytes accessed | tf_op | source)
XLA Modules:
  0.0 60.7 jit_solution(3252695094109235378)
XLA Ops:
  0.0 58.8 %residual_kernel.1 = bf16[512,512]{1,0:T(8,128)(2,1)} custom-call(s32[4,4]{1,0:T(4,128)} %mask_hbm.1, bf16[512,512]{1,0:T(8,128)(2,1)} %amp_hbm.1, bf16[64,512]{1,0:T(8,128)(2,1)} %bitcast.1, bf16[512,512]{1,0:T(8,128)(2,1)} %right_hbm.1, bf16[512,512]{1,0:T(8,128)(2,1)} %left_hbm.1), custom_call_target="tpu_custom_call" | custom-call | flops 2684354560 | bytes 2621440 | tf_op jit(solution)/shard_map/residual_kernel/pallas_call | solution.py:407
  58.8 1.9 %copy.7 = bf16[512,512]{1,0:T(8,128)(2,1)} copy(bf16[512,512]{1,0:T(8,128)(2,1)} %residual_kernel.1) | data formatting | bytes 1048576

commit v5 on v4

--- a/solution.py
+++ b/solution.py
@@ -115,10 +115,10 @@
             here = (slice(i * CH, (i + 1) * CH), slice(v * TB, (v + 1) * TB))
             m[(0, *here)] = (amp[here].astype(f32) * mask[i * CH // TB, v].astype(f32)).astype(bf16)
 
+    answer()
     mask_in.wait()
     masked(from_ends[0])
     masked(from_ends[1])
-    answer()
     met("z")
 
     def m_rows(up, ch):
@@ -351,9 +351,9 @@
     zm(1, 0)
     met("t")
     l0_second()
-    m_own(*range(EARLY, NCH))
     met("x")
     h2_send()
+    m_own(*range(EARLY, NCH))
     zm(1, 1)
     h3_send()
     l1_send(0)

time: 60.9 us -> 60.7 us (level)
  no operation moved by 1% of the time
where the time goes in v5:
time: 60.7 us; the launch traced here: 60.6 us
  Pallas kernels  58.7 us (97%)
  local copies, waits for them, and re-layouts  1.87 us (3%)
    pallas_call x1, Pallas kernels, body(): pl.pallas_call(kernel, out_shape=jax.ShapeDtypeStruct((NB, NB), bf16), in...  58.7 us
    unnamed x1, local copies, waits for them, and re-layouts  1.87 us

profile of v5, /device:TPU:1, one launch (start us, length us, event | category | flops | bytes accessed | tf_op | source)
XLA Modules:
  0.0 60.6 jit_solution(14768940527825177483)
XLA Ops:
  0.0 58.7 %residual_kernel.1 = bf16[512,512]{1,0:T(8,128)(2,1)} custom-call(s32[4,4]{1,0:T(4,128)} %mask_hbm.1, bf16[512,512]{1,0:T(8,128)(2,1)} %amp_hbm.1, bf16[64,512]{1,0:T(8,128)(2,1)} %bitcast.1, bf16[512,512]{1,0:T(8,128)(2,1)} %right_hbm.1, bf16[512,512]{1,0:T(8,128)(2,1)} %left_hbm.1), custom_call_target="tpu_custom_call" | custom-call | flops 2684354560 | bytes 2621440 | tf_op jit(solution)/shard_map/residual_kernel/pallas_call | solution.py:407
  58.7 1.9 %copy.7 = bf16[512,512]{1,0:T(8,128)(2,1)} copy(bf16[512,512]{1,0:T(8,128)(2,1)} %residual_kernel.1) | data formatting | bytes 1048576
